TPU v7x, 32 devices: a whole 2x2x4 slice. The times are simulated.
32 devices in a mesh: wide: 4 (over z), qa: 4 (over y, x), qb: 2 (over core).
Axes of the slice: x: 2, y: 2, z: 4, core: 2. Of those that a mesh axis runs over, the one named last changes fastest.
Arguments:
- core_slices: float32 [32768, 256], P(('wide', 'qa', 'qb')), may hold values from -64 to 64
- next_core: float32 [256, 16384], P('wide', ('qa', 'qb')), may hold values from -0.375 to 0.375
Outputs:
- ortho_basis: float32 [32768, 256], P(('wide', 'qa', 'qb'))
- new_core: float32 [256, 16384], P('wide', ('qa', 'qb'))
All inputs are finite; a program needn't handle non-finite values.
Results may differ from a plain program's by a relative error of at most 0.0003.
Values sent between devices are 32-bit elements; how exact they have to be, the bound alone decides.
A program may use at most 128 MiB of HBM per device.

v0:
```python
import jax
import jax.numpy as jnp
from jax import lax
from jax.sharding import PartitionSpec as P


def leaf_parts(gram):
    count = gram.shape[0]
    places = jnp.arange(count)
    work = gram
    lower = jnp.zeros_like(gram)
    for k in range(count):
        column = work[:, k]
        column = jnp.where(places >= k, column / jnp.sqrt(column[k]), jnp.zeros_like(column))
        work = work - column[:, None] * column[None, :]
        lower = lower.at[:, k].set(column)
    inverse = jnp.zeros_like(gram)
    for k in range(count):
        row = lower[k]
        earlier = jnp.where(places < k, row, jnp.zeros_like(row))
        unit = jnp.where(places == k, jnp.ones_like(row), jnp.zeros_like(row))
        carried = jnp.dot(
            earlier, inverse, precision=lax.Precision.HIGHEST, preferred_element_type=gram.dtype
        )
        inverse = inverse.at[k].set((unit - carried) / row[k])
    return (lower, inverse)


def lower_parts(gram):
    count = gram.shape[0]
    if count <= 16:
        return leaf_parts(gram)
    half = count // 2
    lower_top, inverse_top = lower_parts(gram[:half, :half])
    lower_side = jnp.dot(
        gram[half:, :half],
        inverse_top.T,
        precision=lax.Precision.HIGHEST,
        preferred_element_type=gram.dtype,
    )
    schur = gram[half:, half:] - jnp.dot(
        lower_side, lower_side.T, precision=lax.Precision.HIGHEST, preferred_element_type=gram.dtype
    )
    lower_end, inverse_end = lower_parts(schur)
    inverse_side = -jnp.dot(
        jnp.dot(
            inverse_end,
            lower_side,
            precision=lax.Precision.HIGHEST,
            preferred_element_type=gram.dtype,
        ),
        inverse_top,
        precision=lax.Precision.HIGHEST,
        preferred_element_type=gram.dtype,
    )
    zeros_block = jnp.zeros((half, count - half), gram.dtype)
    lower = jnp.concatenate(
        [
            jnp.concatenate([lower_top, zeros_block], axis=1),
            jnp.concatenate([lower_side, lower_end], axis=1),
        ],
        axis=0,
    )
    inverse = jnp.concatenate(
        [
            jnp.concatenate([inverse_top, zeros_block], axis=1),
            jnp.concatenate([inverse_side, inverse_end], axis=1),
        ],
        axis=0,
    )
    return (lower, inverse)


def upper_factor(gram):
    lower, inverse_lower = lower_parts(gram)
    return (lower.T, inverse_lower.T)


def gram_total(partial_value):
    summed = lax.psum(partial_value, "wide")
    summed = lax.psum(summed, "qa")
    return lax.psum(summed, "qb")


def per_device(core_slices, next_core):
    total_rows = (
        core_slices.shape[0] * lax.axis_size("wide") * lax.axis_size("qa") * lax.axis_size("qb")
    )
    halved = core_slices.astype(jnp.bfloat16)
    first_gram = (
        gram_total(
            lax.dot_general(
                halved, halved, (((0,), (0,)), ((), ())), preferred_element_type=jnp.float32
            )
        )
        / total_rows
    )
    upper_one, inverse_one = upper_factor(first_gram)
    section_one = jnp.dot(
        core_slices,
        inverse_one,
        precision=lax.Precision.HIGHEST,
        preferred_element_type=jnp.float32,
    )
    second_part = lax.dot_general(
        section_one,
        section_one,
        (((0,), (0,)), ((), ())),
        precision=lax.Precision.HIGHEST,
        preferred_element_type=jnp.float32,
    )
    second_gram = gram_total(second_part) / total_rows
    upper_two, inverse_two = upper_factor(second_gram)
    ortho_basis = jnp.dot(
        section_one,
        inverse_two,
        precision=lax.Precision.HIGHEST,
        preferred_element_type=jnp.float32,
    )
    factor = jnp.dot(
        upper_two, upper_one, precision=lax.Precision.HIGHEST, preferred_element_type=jnp.float32
    )
    own_rows = next_core.shape[0]
    own_start = lax.axis_index("wide") * own_rows
    factor_mine = lax.dynamic_slice_in_dim(factor, own_start, own_rows, 0)
    new_core = jnp.dot(
        factor_mine,
        lax.all_gather(next_core, "wide", axis=0, tiled=True),
        precision=lax.Precision.HIGHEST,
        preferred_element_type=jnp.float32,
    )
    return (ortho_basis, new_core)


def solution(mesh):
    return jax.shard_map(
        per_device,
        mesh=mesh,
        in_specs=(P(("wide", "qa", "qb"), None), P("wide", ("qa", "qb"))),
        out_specs=(P(("wide", "qa", "qb"), None), P("wide", ("qa", "qb"))),
        check_vma=False,
    )
```

profile of v0, /device:TPU:0, one launch (start us, length us, event | category | flops | bytes accessed | tf_op | source)
XLA Modules:
  0.0 1880.1 jit_solution(11843121643466913984)
XLA Ops:
  7.2 2.7 fusion.1441
  9.9 39.0 %all-reduce.131.cloned.1.call-done = f32[256,256]{1,0:T(8,128)} async-done(((f32[256,256]{1,0:T(8,128)}), f32[256,256]{1,0:T(8,128)}) %all-reduce.131.cloned.1.call-update) | async-done | bytes 262160 | tf_op jit(solution)/shard_map/psum | solution.py:80
  49.0 45.8 %all-reduce.133.cloned.1.call-done = f32[256,256]{1,0:T(8,128)} async-done(((f32[256,256]{1,0:T(8,128)}), f32[256,256]{1,0:T(8,128)}) %all-reduce.133.cloned.1.call-update) | async-done | bytes 262160 | tf_op jit(solution)/shard_map/psum | solution.py:81
  105.2 10.3 all-reduce.135.cloned.1.call-done
  155.2 1.4 fusion.484
  156.7 1.5 fusion.486
  158.2 1.4 fusion.488
  159.6 1.5 fusion.490
  161.2 1.4 fusion.492
  162.6 1.5 fusion.494
  164.1 1.4 fusion.496
  165.5 1.4 fusion.498
  167.0 1.4 fusion.500
  168.4 1.5 fusion.502
  169.9 1.5 fusion.504
  171.4 1.4 fusion.506
  172.8 1.5 fusion.508
  174.3 1.5 fusion.510
  265.3 1.4 fusion.544
  266.8 1.4 fusion.546
  268.2 1.4 fusion.548
  269.7 1.5 fusion.550
  272.6 1.5 fusion.554
  275.6 1.4 fusion.558
  277.0 1.4 fusion.560
  278.5 1.4 fusion.562
  279.9 1.4 fusion.564
  281.4 1.4 fusion.566
  282.8 1.5 fusion.568
  284.3 1.5 fusion.570
  943.8 1.7 fusion.7092
  945.6 36.6 %all-reduce.137.cloned.1.call-done = f32[256,256]{1,0:T(8,128)} async-done(((f32[256,256]{1,0:T(8,128)}), f32[256,256]{1,0:T(8,128)}) %all-reduce.137.cloned.1.call-update) | async-done | bytes 262160 | tf_op jit(solution)/shard_map/psum | solution.py:80
  982.3 45.4 %all-reduce.139.cloned.1.call-done = f32[256,256]{1,0:T(8,128)} async-done(((f32[256,256]{1,0:T(8,128)}), f32[256,256]{1,0:T(8,128)}) %all-reduce.139.cloned.1.call-update) | async-done | bytes 262160 | tf_op jit(solution)/shard_map/psum | solution.py:81
  1029.2 19.1 %all-reduce.141.cloned.1.call-done = f32[256,256]{1,0:T(8,128)} async-done(((f32[256,256]{1,0:T(8,128)}), f32[256,256]{1,0:T(8,128)}) %all-reduce.141.cloned.1.call-update) | async-done | bytes 262160 | tf_op jit(solution)/shard_map/psum | solution.py:82
  1087.8 1.5 fusion.964
  1089.3 1.5 fusion.966
  1090.9 1.4 fusion.968
  1092.3 1.5 fusion.970
  1093.8 1.5 fusion.972
  1095.3 1.5 fusion.974
  1098.3 1.4 fusion.978
  1099.8 1.4 fusion.980
  1102.6 1.4 fusion.984
  1104.1 1.4 fusion.986
  1105.6 1.5 fusion.988
  1107.0 1.4 fusion.990
  1866.5 2.8 fusion.1481
  1869.3 3.8 fusion.1582
  (3727 shorter events, 1241.8 us)
Async XLA Ops:
  7.2 41.8 %all-reduce.131.cloned.1.call-start = ((), (), s32[]{:S(2)}) async-start(), calls=%async_computation | async-start | bytes 524288 | tf_op jit(solution)/shard_map/psum | solution.py:80
  9.9 85.0 %all-reduce.133.cloned.1.call-start = ((), (), s32[]{:S(2)}) async-start(), calls=%async_computation.1 | async-start | bytes 524288 | tf_op jit(solution)/shard_map/psum | solution.py:81
  49.0 66.5 %all-reduce.135.cloned.1.call-start = ((), (), s32[]{:S(2)}) async-start(), calls=%async_computation.2 | async-start | bytes 524288 | tf_op jit(solution)/shard_map/psum | solution.py:82
  94.9 887.4 %all-reduce.137.cloned.1.call-start = ((), (), s32[]{:S(2)}) async-start(), calls=%async_computation.3 | async-start | bytes 524288 | tf_op jit(solution)/shard_map/psum | solution.py:80
  153.1 2.1 copy-start.5
  263.2 2.1 copy-start.1
  851.5 91.2 %copy-start = (f32[1024,256]{1,0:T(8,128)S(1)}, f32[1024,256]{1,0:T(8,128)}, u32[]{:S(2)}) copy-start(f32[1024,256]{1,0:T(8,128)} %param.2050) | copy-start | bytes 3145732
  943.8 85.0 %copy-start.6 = (f32[16,16]{1,0:T(8,128)S(1)}, f32[16,16]{1,0:T(8,128)}, u32[]{:S(2)}) copy-start(f32[16,16]{1,0:T(8,128)} %copy-done.5) | copy-start | bytes 3076
  943.8 85.2 %copy-start.2 = (f32[16,16]{1,0:T(8,128)S(1)}, f32[16,16]{1,0:T(8,128)}, u32[]{:S(2)}) copy-start(f32[16,16]{1,0:T(8,128)} %copy-done.1) | copy-start | bytes 3076
  945.6 82.2 %all-reduce.139.cloned.1.call-start = ((), (), s32[]{:S(2)}) async-start(), calls=%async_computation.4 | async-start | bytes 524288 | tf_op jit(solution)/shard_map/psum | solution.py:81
  982.3 66.0 %all-reduce.141.cloned.1.call-start = ((), (), s32[]{:S(2)}) async-start(), calls=%async_computation.5 | async-start | bytes 524288 | tf_op jit(solution)/shard_map/psum | solution.py:82
  1027.8 841.6 %all-gather.2.cloned.1.call-start = ((), (), s32[]{:S(2)}) async-start(), calls=%async_computation.6 | async-start | bytes 2621440 | tf_op jit(solution)/shard_map/all_gather | solution.py:128
  1085.7 2.1 copy-start.3
  1761.7 102.4 %copy-start.4 = (f32[16,16]{1,0:T(8,128)S(1)}, f32[16,16]{1,0:T(8,128)}, u32[]{:S(2)}) copy-start(f32[16,16]{1,0:T(8,128)} %copy-done.3) | copy-start | bytes 3076
Sparse Core Ops, SparseCore 0:
  10.9 38.0 all-reduce.130
  52.2 42.6 all-reduce.132
  97.2 18.2 all-reduce.134
  945.7 36.5 all-reduce.136
  985.0 42.6 all-reduce.138
  1030.0 18.2 all-reduce.140
  1049.9 47.1 all-gather.1
where the time goes:
time: 1900 us; the launch traced here: 1880 us
  other arithmetic  470 us (25%)
  matrix products  425 us (22%)
  local copies, waits for them, and re-layouts  412 us (22%)
  between operations  376 us (20%)
  waiting for transfers between devices  197 us (10%)
    dot_general x481, matrix products, leaf_parts(): jnp.dot(earlier, inverse, precision=lax.Precision.HIGHEST, preferred_elem...  394 us
    select_n x928, other arithmetic, leaf_parts(): jnp.where(places >= k, column / jnp.sqrt(column[k]), jnp.zeros_like(column))  369 us
    slice x512, local copies, waits for them, and re-layouts, leaf_parts(): column[k]  297 us
    psum x2, waiting for transfers between devices, gram_total(): summed = lax.psum(summed, 'qa')  91.2 us
    psum x2, waiting for transfers between devices, gram_total(): summed = lax.psum(partial_value, 'wide')  75.7 us
    scatter x512, local copies, waits for them, and re-layouts, leaf_parts(): lower = lower.at[:, k].set(column)  61 us
    sub x480, other arithmetic, leaf_parts(): work = work - column[:, None] * column[None, :]  42.9 us
    slice x64, local copies, waits for them, and re-layouts, leaf_parts(): inverse = inverse.at[k].set((unit - carried) / row[k])  40.7 us
  transfers between devices with their start and end apart: 7, of which 6 were waited for; matrix products, arithmetic and copies ran while one was open for 35% of the time, Pallas kernels for 0%

commit v1 on v0

v1 whole, which is shorter than its diff:
```python
import functools

import jax
import jax.numpy as jnp
from jax import lax
from jax.experimental import pallas as pl
from jax.experimental.pallas import tpu as pltpu
from jax.sharding import PartitionSpec as P

AXES = ("wide", "qa", "qb")
STRIP = 8
LANES = 128
PANEL = 32
HIGHEST = lax.Precision.HIGHEST
VMEM_LIMIT = 40 * 1024 * 1024


def mm(a, b, dims):
    return lax.dot_general(
        a, b, (dims, ((), ())), precision=HIGHEST, preferred_element_type=jnp.float32
    )


def forward(items, below, inverse_diag):
    done = []
    for j in range(STRIP):
        value = items[j]
        for m in range(j):
            value = value - below[j, m] * done[m]
        done.append(value * inverse_diag[j])
    return done


def factor_in_place(work, upper):
    n = work.shape[0]
    tiles = n // LANES

    def wide(value):
        return jnp.concatenate([value] * tiles, axis=1) if tiles > 1 else value

    lane = lax.broadcasted_iota(jnp.int32, (STRIP, n), 1)
    sub = lax.broadcasted_iota(jnp.int32, (STRIP, n), 0)

    def stack(rows):
        out = rows[0]
        for i in range(1, STRIP):
            out = jnp.where(sub == i, rows[i], out)
        return out

    for p in range(0, n, PANEL):
        count = PANEL // STRIP
        strips = [work[p + STRIP * s : p + STRIP * (s + 1), :] for s in range(count)]
        uppers, fulls = [], []
        for s in range(count):
            k = p + STRIP * s
            here = strips[s]
            inside = (lane >= k) & (lane < k + STRIP)
            spread = [jnp.broadcast_to(here[i : i + 1, :], (STRIP, n)) for i in range(STRIP)]
            a = {}
            for j in range(STRIP):
                for i in range(j, STRIP):
                    a[i, j] = jnp.broadcast_to(
                        spread[j][:, k + i : k + i + 1], (STRIP, LANES)
                    )
            below, inverse_diag = {}, []
            for j in range(STRIP):
                d = a[j, j]
                r = lax.rsqrt(d)
                r = r * (1.5 - 0.5 * d * r * r)
                inverse_diag.append(r)
                for i in range(j + 1, STRIP):
                    below[i, j] = a[i, j] * r
                for i in range(j + 1, STRIP):
                    for m in range(j + 1, i + 1):
                        a[i, m] = a[i, m] - below[i, j] * below[m, j]
            below_w = {key: wide(value) for key, value in below.items()}
            diag_w = [wide(value) for value in inverse_diag]
            u_rows = forward(spread, below_w, diag_w)
            x_rows = forward(
                [
                    jnp.where(inside, jnp.where(lane == k + i, 1.0, 0.0), spread[i])
                    for i in range(STRIP)
                ],
                below_w,
                diag_w,
            )
            full = stack(x_rows)
            uppers.append(jnp.where(lane >= k + sub, stack(u_rows), 0.0))
            fulls.append(jnp.where((lane >= k + STRIP) & (lane < p + PANEL), 0.0, full))
            for t in range(s + 1, count):
                other = strips[t]
                side = forward(
                    [
                        jnp.broadcast_to(other[:, k + j : k + j + 1], (STRIP, LANES))
                        for j in range(STRIP)
                    ],
                    below,
                    inverse_diag,
                )
                value = jnp.where(inside, 0.0, other)
                for j in range(STRIP):
                    value = value - wide(side[j]) * x_rows[j]
                strips[t] = value
        end = p + PANEL
        u_panel = jnp.concatenate(uppers, axis=0)
        x_panel = jnp.concatenate(fulls, axis=0)
        upper[p:end, :] = u_panel
        lane_panel = lax.broadcasted_iota(jnp.int32, (PANEL, n), 1)
        work[p:end, :] = jnp.where(lane_panel < end, x_panel, 0.0)
        if end < n:
            start = end // LANES * LANES
            update = mm(u_panel[:, start:], x_panel, ((0,), (0,)))[end - start :, :]
            rest_lane = lax.broadcasted_iota(jnp.int32, (n - end, n), 1)
            rest = work[end:, :]
            rest = jnp.where((rest_lane >= p) & (rest_lane < end), 0.0, rest)
            work[end:, :] = rest - update


def first_kernel(total_rows, core_ref, gram_ref, section_ref, part_ref, upper_ref, work):
    work[...] = gram_ref[...] / total_rows
    factor_in_place(work, upper_ref)
    section_ref[...] = mm(core_ref[...], work[...], ((1,), (1,)))
    part_ref[...] = mm(section_ref[...], section_ref[...], ((0,), (0,)))


def second_kernel(
    total_rows, section_ref, gram_ref, upper_one_ref, next_ref, ortho_ref, new_ref, work, upper
):
    rows, columns = new_ref.shape
    work[...] = gram_ref[...] / total_rows
    factor_in_place(work, upper)
    ortho_ref[...] = mm(section_ref[...], work[...], ((1,), (1,)))
    start = pl.multiple_of(lax.axis_index("wide") * rows, rows)
    mine = mm(upper[pl.ds(start, rows), :], upper_one_ref[...], ((1,), (0,)))
    tile = min(512, columns)
    for c in range(0, columns, tile):
        new_ref[:, c : c + tile] = mm(mine, next_ref[:, c : c + tile], ((1,), (0,)))


def vmem_specs(count):
    return [pl.BlockSpec(memory_space=pltpu.VMEM)] * count


def gram_total(part):
    return lax.psum(part, AXES)


def per_device(core_slices, next_core):
    rows, rank = core_slices.shape
    f32 = jnp.float32
    total_rows = rows * lax.axis_size("wide") * lax.axis_size("qa") * lax.axis_size("qb")
    square = jax.ShapeDtypeStruct((rank, rank), f32)
    block = jax.ShapeDtypeStruct((rows, rank), f32)
    params = pltpu.CompilerParams(vmem_limit_bytes=VMEM_LIMIT)
    gathered = lax.all_gather(next_core, "wide", axis=0, tiled=True)
    halved = core_slices.astype(jnp.bfloat16)
    first_gram = gram_total(
        lax.dot_general(halved, halved, (((0,), (0,)), ((), ())), preferred_element_type=f32)
    )
    section, part, upper_one = pl.pallas_call(
        functools.partial(first_kernel, total_rows),
        out_shape=(block, square, square),
        in_specs=vmem_specs(2),
        out_specs=tuple(vmem_specs(3)),
        scratch_shapes=[pltpu.VMEM((rank, rank), f32)],
        compiler_params=params,
        name="factor_one",
    )(core_slices, first_gram)
    second_gram = gram_total(part)
    ortho_basis, new_core = pl.pallas_call(
        functools.partial(second_kernel, total_rows),
        out_shape=(block, jax.ShapeDtypeStruct(next_core.shape, f32)),
        in_specs=vmem_specs(4),
        out_specs=tuple(vmem_specs(2)),
        scratch_shapes=[pltpu.VMEM((rank, rank), f32), pltpu.VMEM((rank, rank), f32)],
        compiler_params=params,
        name="factor_two",
    )(section, second_gram, upper_one, gathered)
    return ortho_basis, new_core


def solution(mesh):
    return jax.shard_map(
        per_device,
        mesh=mesh,
        in_specs=(P(AXES, None), P("wide", ("qa", "qb"))),
        out_specs=(P(AXES, None), P("wide", ("qa", "qb"))),
        check_vma=False,
    )
```

time: 1900 us -> 333 us (0.18); the launches traced: 1880 us -> 333 us
  other arithmetic: 470 us -> 0 us
  matrix products: 425 us -> 2.77 us
  local copies, waits for them, and re-layouts: 412 us -> 3.49 us
  between operations: 376 us -> 15.5 us
  waiting for transfers between devices: 197 us -> 282 us
  Pallas kernels: 0 us -> 28.4 us
    dot_general x606 -> x0, matrix products: 422 us -> none  [the longest x481 394 us: leaf_parts(): jnp.dot(earlier, inverse, precision=lax.Precision.HIGHEST, preferred_elem...]
    select_n x928 -> x0, other arithmetic: 369 us -> none  [leaf_parts(): jnp.where(places >= k, column / jnp.sqrt(column[k]), jnp.zeros_like(column))]
    slice x576 -> x0, local copies, waits for them, and re-layouts: 338 us -> none  [the longest x512 297 us: leaf_parts(): column[k]]
    psum x6 -> x2, waiting for transfers between devices: 196 us -> 282 us  [gram_total(): return lax.psum(part, AXES)]
    scatter x1024 -> x0, local copies, waits for them, and re-layouts: 74.4 us -> none  [the longest x512 61 us: leaf_parts(): lower = lower.at[:, k].set(column)]
    sub x480 -> x0, other arithmetic: 42.9 us -> none  [leaf_parts(): work = work - column[:, None] * column[None, :]]
    another operation x47 -> x0, other arithmetic: 29.3 us -> none
    pallas_call x0 -> x2, Pallas kernels: none -> 28.4 us  [the longest x1 14.7 us: per_device(): pl.pallas_call(functools.partial(first_kernel, total_rows), out_shape=(bl...]
  transfers between devices with their start and end apart: 7 -> 3, of which waited for: 6 -> 2; matrix products, arithmetic and copies ran while one was open for 35% -> 0% of each run, Pallas kernels for 0% -> 0%
where the time goes in v1:
time: 333 us
  waiting for transfers between devices  282 us (85%)
  Pallas kernels  28.4 us (9%)
  between operations  15.5 us (5%)
  local copies, waits for them, and re-layouts  3.49 us (1%)
    psum x2, waiting for transfers between devices, gram_total(): return lax.psum(part, AXES)  282 us
    pallas_call x1, Pallas kernels, per_device(): pl.pallas_call(functools.partial(first_kernel, total_rows), out_shape=(bl...  14.7 us
    pallas_call x1, Pallas kernels, per_device(): pl.pallas_call(functools.partial(second_kernel, total_rows), out_shape=(b...  13.7 us
  transfers between devices with their start and end apart: 3, of which 2 were waited for; matrix products, arithmetic and copies ran while one was open for 0% of the time, Pallas kernels for 0%

profile of v1, /device:TPU:0, one launch (start us, length us, event | category | flops | bytes accessed | tf_op | source)
XLA Modules:
  0.0 332.9 jit_solution(9488371708410065417)
XLA Ops:
  8.0 0.0 copy-start
  8.0 0.0 all-reduce.3.cloned.1.call-start
  8.1 2.8 fusion
  10.8 0.0 all-reduce.3.cloned.1.call-update
  10.8 0.0 all-reduce.5.cloned.1.call-start
  10.9 131.7 %all-reduce.3.cloned.1.call-done.gram_ref = f32[256,256]{1,0:T(8,128)} async-done(((f32[256,256]{1,0:T(8,128)}), f32[256,256]{1,0:T(8,128)}) %all-reduce.3.cloned.1.call-update) | async-done | bytes 262160 | tf_op jit(solution)/shard_map/psum | solution.py:145
  142.6 0.0 copy-done
  142.6 0.0 copy-start.3
  142.6 0.9 copy-done.3
  143.5 14.7 %factor_one.1 = (f32[1024,256]{1,0:T(8,128)S(1)}, f32[256,256]{1,0:T(8,128)}, f32[256,256]{1,0:T(8,128)S(1)}) custom-call(f32[1024,256]{1,0:T(8,128)S(1)} %copy-done, f32[256,256]{1,0:T(8,128)S(1)} %copy-done.3), custom_call_target="tpu_custom_call" | custom-call | tf_op jit(solution)/shard_map/factor_one/pallas_call | solution.py:160
  158.2 0.0 all-reduce.5.cloned.1.call-update
  158.2 0.2 all-gather.2.cloned.1.call-start
  158.4 0.3 all-gather.2.cloned.1.call-update
  158.8 150.4 %all-reduce.5.cloned.1.call-done.gram_ref = f32[256,256]{1,0:T(8,128)} async-done(((f32[256,256]{1,0:T(8,128)}), f32[256,256]{1,0:T(8,128)}) %all-reduce.5.cloned.1.call-update) | async-done | bytes 262160 | tf_op jit(solution)/shard_map/psum | solution.py:145
  309.2 0.0 all-gather.2.cloned.1.call-done.next_ref
  309.2 0.0 copy-start.1
  309.2 1.6 copy-done.1
  310.8 0.0 copy-start.2
  310.8 0.9 copy-done.2
  311.7 13.7 %factor_two.1 = (f32[1024,256]{1,0:T(8,128)}, f32[64,2048]{1,0:T(8,128)}) custom-call(f32[1024,256]{1,0:T(8,128)S(1)} %get-tuple-element.5.section_ref, f32[256,256]{1,0:T(8,128)S(1)} %copy-done.2, f32[256,256]{1,0:T(8,128)S(1)} %get-tuple-element.7.upper_one_ref, f32[256,2048]{1,0:T(8,128)S(1)} %copy-done.1), custom_call_target="tpu_custom_call" | custom-call | tf_op jit(solution)/shard_map/factor_two/pallas_call | solution.py:170
Async XLA Ops:
  8.0 134.6 %copy-start = (f32[1024,256]{1,0:T(8,128)S(1)}, f32[1024,256]{1,0:T(8,128)}, u32[]{:S(2)}) copy-start(f32[1024,256]{1,0:T(8,128)} %core_ref.1) | copy-start | bytes 3145732
  8.0 134.6 %all-reduce.3.cloned.1.call-start = ((), (), s32[]{:S(2)}) async-start(), calls=%async_computation | async-start | bytes 524288 | tf_op jit(solution)/shard_map/psum | solution.py:145
  10.8 298.3 %all-reduce.5.cloned.1.call-start = ((), (), s32[]{:S(2)}) async-start(), calls=%async_computation.1 | async-start | bytes 524288 | tf_op jit(solution)/shard_map/psum | solution.py:145
  142.6 1.0 copy-start.3
  158.2 151.0 %all-gather.2.cloned.1.call-start = ((), (), s32[]{:S(2)}) async-start(), calls=%async_computation.2 | async-start | bytes 2621440 | tf_op jit(solution)/shard_map/all_gather | solution.py:155
  309.2 1.6 copy-start.1
  310.8 0.9 copy-start.2
Sparse Core Ops, SparseCore 0:
  14.9 127.6 all-reduce.2
  158.3 150.7 all-reduce.4
Sparse Core Ops, SparseCore 1:
  160.3 45.1 all-gather.1
